TPU v7x, 256 devices: a whole 4x4x8 slice. The times are simulated.
256 devices in a mesh: sub: 64 (over z, y, x_hi), rng: 4 (over x_lo, core).
Axes of the slice: x: 4 (x_hi: 2, x_lo: 2; x = x_hi * 2 + x_lo), y: 4, z: 8, core: 2. Of those that a mesh axis runs over, the one named last changes fastest.
Arguments:
- images: bfloat16 [2, 128, 1024, 256], P(None, 'sub', 'rng'), may hold values from -6 to 6
- beam_index: int32 [2, 7680], replicated, may hold values from 0 to 2044, as said below
- range_shift: int32 [2, 7680], replicated, may hold values from -2 to 2
- tap_weights: bfloat16 [2, 4, 7680], replicated, may hold values from -2 to 2
- phase_base: float32 [2, 7680], replicated, may hold values from -3.140625 to 3.140625
- phase_slope: float32 [2, 7680], replicated, may hold values from -0.05 to 0.05
Outputs:
- final: bfloat16 [2, 64, 4, 32, 4096], P(None, 'sub', 'rng')
Inputs may be any that keep to these rules, and one draw needn't show every extreme that they name: `beam_index`: for output beam j of a section whose input images have W beams, the entry lies within j // 2 - 3 to j // 2 - 1, clipped to 0 .. W - 4.
All inputs are finite; a program needn't handle non-finite values.
Results may differ from a plain program's by a relative error of at most 0.0064.
Values may be sent and summed in bfloat16 or wider, within the bound.
A program may use at most 64 MiB of HBM per device.

v0:
```python
import functools

import jax
import jax.numpy as jnp
from jax import lax
from jax.experimental import pallas as pl
from jax.experimental.pallas import tpu as pltpu
from jax.sharding import PartitionSpec as P

MESH = pl.DeviceIdType.MESH
BF16 = jnp.bfloat16
F32 = jnp.float32
CHIPS = 8
COLUMN = 8
STRIPS = 4
STRIP = 256
TILE = 32
HALO = 8
BLOCK = TILE + 2 * HALO
BEAMS = 256
LANES = 128
TAPS = 4
SHIFT = 2
TILES = (4, 10, 18, 34)
FIRST = (0, 4, 14, 32)
TABLE = (0, 4, 12, 28)
BAND_ROWS = 96


def build_tables(z, q, idx, shf, wts, base, slope, band, cos_t, sin_t):
    start = (q * STRIP + z * TILE - HALO).astype(F32)
    iota8 = lax.broadcasted_iota(jnp.int32, (8, LANES), 0).astype(F32)
    iota_k = lax.broadcasted_iota(jnp.int32, (BAND_ROWS, LANES), 0)

    def one(child, tile, col, origin, offset):
        band[child, tile] = jnp.zeros((BEAMS, LANES), BF16)
        cols = pl.ds(col, LANES)
        first = idx[child : child + 1, cols] - (origin + offset)
        weights = wts[child, :, cols].astype(F32)
        patch = jnp.zeros((BAND_ROWS, LANES), F32)
        for tap in range(TAPS):
            patch = jnp.where(iota_k == first + tap, weights[tap : tap + 1, :], patch)
        if not isinstance(offset, int):
            offset = pl.multiple_of(offset, 16)
        band[child, tile, pl.ds(offset, BAND_ROWS), :] = patch.astype(BF16)
        rate = slope[child : child + 1, cols]
        theta = base[child : child + 1, cols] + rate * (start + iota8)
        c, s = jnp.cos(theta), jnp.sin(theta)
        turn = jnp.broadcast_to(rate * 8.0, (8, LANES))
        c8, s8 = jnp.cos(turn), jnp.sin(turn)
        for step in range(BLOCK // 8):
            cos_t[child, tile, step * 8 : step * 8 + 8, :] = c
            sin_t[child, tile, step * 8 : step * 8 + 8, :] = s
            c, s = c * c8 - s * s8, s * c8 + c * s8

    for child in range(2):
        for tile in range(TILES[0]):
            one(child, tile, tile * LANES, 0, (0, 48, 112, 160)[tile])
    for section in range(1, 4):
        last = TILES[section] - 1
        for child in range(2):
            for pad in (0, last):
                band[child, FIRST[section] + pad] = jnp.zeros((BEAMS, LANES), BF16)
                cos_t[child, FIRST[section] + pad] = jnp.zeros((BLOCK, LANES), F32)
                sin_t[child, FIRST[section] + pad] = jnp.zeros((BLOCK, LANES), F32)

        def body(tile, carry, section=section):
            block, side = tile // 2, tile % 2
            for child in range(2):
                one(
                    child,
                    FIRST[section] + tile,
                    pl.multiple_of((TABLE[section] + tile - 1) * LANES, LANES),
                    LANES * (block - 1),
                    48 + 64 * side,
                )
            return carry

        lax.fori_loop(1, last, body, 0)


def masks_of(shf, col):
    found = []
    for child in range(2):
        row = jnp.broadcast_to(shf[child : child + 1, pl.ds(col, LANES)], (16, LANES))
        found.append({o: row == o for o in (-2, -1, 1, 2)})
    return found


def merged_rows(v, slot, masks, cos_t, sin_t, tile, row):
    moved = []
    for child in range(2):
        for plane in range(2):
            at = HALO + row
            u = v[child, plane, slot, at : at + 16, :]
            for o in (-2, -1, 1, 2):
                u = jnp.where(masks[child][o], v[child, plane, slot, at + o : at + o + 16, :], u)
            moved.append(u)
    c0, s0 = cos_t[0, tile, row : row + 16, :], sin_t[0, tile, row : row + 16, :]
    c1, s1 = cos_t[1, tile, row : row + 16, :], sin_t[1, tile, row : row + 16, :]
    real = (c0 * moved[0] - s0 * moved[1]) + (c1 * moved[2] - s1 * moved[3])
    imag = (s0 * moved[0] + c0 * moved[1]) + (s1 * moved[2] + c1 * moved[3])
    return real, imag


def section_zero(image, low, high, recv, shf, band, cos_t, sin_t, v, out):
    iota = lax.broadcasted_iota(jnp.int32, (16, LANES), 0)
    for child in range(2):
        lhs = recv[image, :, child].reshape(2 * BLOCK, BEAMS)
        rhs = jnp.concatenate([band[child, t] for t in range(4)], axis=1)
        product = jnp.dot(lhs, rhs, preferred_element_type=F32)
        for plane in range(2):
            for t in range(4):
                v[child, plane, t, HALO : HALO + BLOCK, :] = product[
                    plane * BLOCK : (plane + 1) * BLOCK, t * LANES : (t + 1) * LANES
                ]
    for t in range(4):
        masks = masks_of(shf, t * LANES)
        for row in range(0, BLOCK, 16):
            real, imag = merged_rows(v, t, masks, cos_t, sin_t, t, row)
            inside = (iota + row >= low) & (iota + row < high)
            cols = slice((t + 1) * LANES, (t + 2) * LANES)
            out[0, image, row : row + 16, cols] = jnp.where(inside, real, 0.0).astype(BF16)
            out[1, image, row : row + 16, cols] = jnp.where(inside, imag, 0.0).astype(BF16)


def section_later(section, low, high, source, shf, band, cos_t, sin_t, v, out):
    images = 8 >> section
    tiles = TILES[section]
    iota = lax.broadcasted_iota(jnp.int32, (16, LANES), 0)

    def block_body(block, carry):
        window = pl.ds(pl.multiple_of(block * LANES, LANES), BEAMS)
        for child in range(2):
            lhs = source[:, child * images : (child + 1) * images, :, window]
            lhs = lhs.reshape(2 * images * BLOCK, BEAMS)
            pair = FIRST[section] + 2 * block
            rhs = jnp.concatenate([band[child, pair], band[child, pair + 1]], axis=1)
            product = jnp.dot(lhs, rhs, preferred_element_type=F32)
            for plane in range(2):
                for image in range(images):
                    at = (plane * images + image) * BLOCK
                    for side in range(2):
                        v[child, plane, 2 * image + side, HALO : HALO + BLOCK, :] = product[
                            at : at + BLOCK, side * LANES : (side + 1) * LANES
                        ]
        for side in range(2):
            tile = 2 * block + side
            known = jnp.clip(tile - 1, 0, tiles - 3)
            masks = masks_of(shf, pl.multiple_of((TABLE[section] + known) * LANES, LANES))
            cols = pl.ds(pl.multiple_of(tile * LANES, LANES), LANES)
            for image in range(images):
                if section < 3:
                    for row in range(0, BLOCK, 16):
                        real, imag = merged_rows(
                            v, 2 * image + side, masks, cos_t, sin_t, FIRST[section] + tile, row
                        )
                        inside = (iota + row >= low) & (iota + row < high)
                        out[0, image, row : row + 16, cols] = jnp.where(inside, real, 0.0).astype(BF16)
                        out[1, image, row : row + 16, cols] = jnp.where(inside, imag, 0.0).astype(BF16)
                else:
                    for row in range(0, TILE, 16):
                        real, imag = merged_rows(
                            v, side, masks, cos_t, sin_t, FIRST[section] + tile, row + HALO
                        )
                        out[0, row : row + 16, cols] = real.astype(BF16)
                        out[1, row : row + 16, cols] = imag.astype(BF16)
        return carry

    lax.fori_loop(0, tiles // 2, block_body, 0)


def kernel(
    images, idx, shf, wts, base, slope, final,
    xin, send, recv, hsend, hrecv, band, cos_t, sin_t, s1, s2, s3, outs, v,
    local_sem, send_sem, recv_sem, hsend_sem, hrecv_sem, comm=True, place=None,
):
    if comm:
        sub, q = lax.axis_index("sub"), lax.axis_index("rng")
        z, lane = sub // COLUMN, sub % COLUMN
    else:
        z, q = place
        z, q = jnp.int32(z), jnp.int32(q)

    def device(zz, qq):
        return (zz * COLUMN + lane, qq)

    if comm:
        barrier = pltpu.get_barrier_semaphore()
        for step in range(1, CHIPS):
            pl.semaphore_signal(
                barrier, inc=1, device_id=device((z + step) % CHIPS, q), device_id_type=MESH
            )

        @pl.when((z == 0) & (q > 0))
        def _():
            for other in range(CHIPS):
                pl.semaphore_signal(
                    barrier, inc=1, device_id=device(other, q - 1), device_id_type=MESH
                )

        @pl.when((z == CHIPS - 1) & (q < STRIPS - 1))
        def _():
            for other in range(CHIPS):
                pl.semaphore_signal(
                    barrier, inc=1, device_id=device(other, q + 1), device_id_type=MESH
                )

        load = pltpu.make_async_copy(images, xin, local_sem)
        load.start()
        load.wait()
        send[0, :, :, 0:HALO, :] = jnp.zeros((2, 2, HALO, BEAMS), BF16)
        send[CHIPS - 1, :, :, BLOCK - HALO :, :] = jnp.zeros((2, 2, HALO, BEAMS), BF16)
        for to in range(CHIPS):
            begin, end = max(TILE * to - HALO, 0), min(TILE * to + TILE + HALO, STRIP)
            at = begin - (TILE * to - HALO)
            send[to, :, :, at : at + end - begin, :] = xin[:, :, begin:end, :]
        for image in range(2):
            rows = slice(image * HALO, (image + 1) * HALO)
            hsend[0, :, rows, :] = xin[:, image, STRIP - HALO :, :]
            hsend[1, :, rows, :] = xin[:, image, 0:HALO, :]
        peers = CHIPS - 1 + (q > 0).astype(jnp.int32) + (q < STRIPS - 1).astype(jnp.int32)
        pl.semaphore_wait(barrier, peers)

        def block_copy(step):
            return pltpu.make_async_remote_copy(
                src_ref=send.at[(z + step) % CHIPS],
                dst_ref=recv.at[z],
                send_sem=send_sem.at[step],
                recv_sem=recv_sem.at[step],
                device_id=device((z + step) % CHIPS, q),
                device_id_type=MESH,
            )

        def halo_copy(side):
            return pltpu.make_async_remote_copy(
                src_ref=hsend.at[side],
                dst_ref=hrecv.at[z],
                send_sem=hsend_sem.at[side],
                recv_sem=hrecv_sem.at[z],
                device_id=device(0, q + 1) if side == 0 else device(CHIPS - 1, q - 1),
                device_id_type=MESH,
            )

        @pl.when(q < STRIPS - 1)
        def _():
            halo_copy(0).start()

        @pl.when(q > 0)
        def _():
            halo_copy(1).start()

        for step in (1, 7, 2, 6, 3, 5, 4):
            block_copy(step).start()
        recv[z] = send[z]
    else:
        load = pltpu.make_async_copy(images, recv, local_sem)
        load.start()
        load.wait()

    build_tables(z, q, idx, shf, wts, base, slope, band, cos_t, sin_t)
    for ref, width in ((s1, 512), (s2, 1024), (s3, 2048)):
        lead = ref.shape[:-1]
        ref[..., 0:LANES] = jnp.zeros(lead + (LANES,), BF16)
        ref[..., LANES + width :] = jnp.zeros(lead + (LANES,), BF16)

    low = jnp.where((z == 0) & (q == 0), HALO, 0)
    high = jnp.where((z == CHIPS - 1) & (q == STRIPS - 1), BLOCK - HALO, BLOCK)

    def arrival(turn, carry):
        step = jnp.where(turn % 2 == 1, (turn + 1) // 2, (CHIPS - turn // 2) % CHIPS)
        image = (z + CHIPS - step) % CHIPS
        if comm:

            @pl.when(turn > 0)
            def _():
                pltpu.make_async_remote_copy(
                    src_ref=send.at[image],
                    dst_ref=recv.at[image],
                    send_sem=send_sem.at[step],
                    recv_sem=recv_sem.at[step],
                    device_id=device(image, q),
                    device_id_type=MESH,
                ).wait_recv()

            def take(rows):
                pltpu.make_async_remote_copy(
                    src_ref=hsend.at[0],
                    dst_ref=hrecv.at[image],
                    send_sem=hsend_sem.at[0],
                    recv_sem=hrecv_sem.at[image],
                    device_id=device(image, q),
                    device_id_type=MESH,
                ).wait_recv()
                for part in range(2):
                    recv[image, :, part, rows, :] = hrecv[
                        image, :, part * HALO : (part + 1) * HALO, :
                    ]

            @pl.when((z == 0) & (q > 0))
            def _():
                take(slice(0, HALO))

            @pl.when((z == CHIPS - 1) & (q < STRIPS - 1))
            def _():
                take(slice(BLOCK - HALO, BLOCK))

        section_zero(image, low, high, recv, shf, band, cos_t, sin_t, v, s1)
        return carry

    lax.fori_loop(0, CHIPS, arrival, 0)
    section_later(1, low, high, s1, shf, band, cos_t, sin_t, v, s2)
    section_later(2, low, high, s2, shf, band, cos_t, sin_t, v, s3)
    section_later(3, low, high, s3, shf, band, cos_t, sin_t, v, outs)

    store = pltpu.make_async_copy(outs.at[:, :, pl.ds(LANES, 4096)], final, local_sem)
    store.start()
    if comm:
        for step in range(1, CHIPS):
            block_copy(step).wait_send()

        @pl.when(q < STRIPS - 1)
        def _():
            halo_copy(0).wait_send()

        @pl.when(q > 0)
        def _():
            halo_copy(1).wait_send()

    store.wait()


def call(images, tables, comm=True, place=None):
    vmem = pl.BlockSpec(memory_space=pltpu.VMEM)
    anywhere = pl.BlockSpec(memory_space=pl.ANY)
    dma = pltpu.SemaphoreType.DMA
    tiles = sum(TILES)
    params = dict(vmem_limit_bytes=48 * 2**20, has_side_effects=True)
    if comm:
        params["collective_id"] = 0
    return pl.pallas_call(
        functools.partial(kernel, comm=comm, place=place),
        out_shape=jax.ShapeDtypeStruct((2, TILE, 4096), BF16),
        in_specs=[anywhere] + [vmem] * 5,
        out_specs=anywhere,
        scratch_shapes=[
            pltpu.VMEM((2, 2, STRIP, BEAMS), BF16),
            pltpu.VMEM((CHIPS, 2, 2, BLOCK, BEAMS), BF16),
            pltpu.VMEM((CHIPS, 2, 2, BLOCK, BEAMS), BF16),
            pltpu.VMEM((2, 2, 2 * HALO, BEAMS), BF16),
            pltpu.VMEM((CHIPS, 2, 2 * HALO, BEAMS), BF16),
            pltpu.VMEM((2, tiles, BEAMS, LANES), BF16),
            pltpu.VMEM((2, tiles, BLOCK, LANES), F32),
            pltpu.VMEM((2, tiles, BLOCK, LANES), F32),
            pltpu.VMEM((2, 8, BLOCK, 512 + 2 * LANES), BF16),
            pltpu.VMEM((2, 4, BLOCK, 1024 + 2 * LANES), BF16),
            pltpu.VMEM((2, 2, BLOCK, 2048 + 2 * LANES), BF16),
            pltpu.VMEM((2, TILE, 4096 + 2 * LANES), BF16),
            pltpu.VMEM((2, 2, 8, BLOCK + 2 * HALO, LANES), F32),
            dma,
            dma((CHIPS,)),
            dma((CHIPS,)),
            dma((2,)),
            dma((CHIPS,)),
        ],
        compiler_params=pltpu.CompilerParams(**params),
    )(images, *tables)


def local(images, *tables):
    return call(images[:, :], tables).reshape(2, 1, 1, TILE, 4096)


def solution(mesh):
    in_specs = (P(None, "sub", "rng", None), P(), P(), P(), P(), P())
    out_specs = P(None, "sub", "rng", None, None)
    return jax.shard_map(local, mesh=mesh, in_specs=in_specs, out_specs=out_specs, check_vma=False)
```

profile of v0, /device:TPU:1, one launch (start us, length us, event | category | flops | bytes accessed | tf_op | source)
XLA Modules:
  0.0 42.7 jit_solution(10753614859900082030)
XLA Ops:
  0.0 0.0 copy-start
  0.0 1.0 %copy-done = bf16[2,2,256,256]{3,2,1,0:T(8,128)(2,1)S(1)} copy-done((bf16[2,2,256,256]{3,2,1,0:T(8,128)(2,1)S(1)}, bf16[2,2,256,256]{3,2,1,0:T(8,128)(2,1)}, u32[]{:S(2)}) %copy-start) | copy-done | bytes 524312
  1.0 0.0 copy-start.1
  1.0 0.9 %copy-done.1 = bf16[2,4,7680]{2,1,0:T(4,128)(2,1)S(1)} copy-done((bf16[2,4,7680]{2,1,0:T(4,128)(2,1)S(1)}, bf16[2,4,7680]{2,1,0:T(4,128)(2,1)}, u32[]{:S(2)}) %copy-start.1) | copy-done | bytes 122904
  1.9 0.0 copy-start.2
  1.9 0.8 %copy-done.2 = s32[2,7680]{1,0:T(2,128)S(1)} copy-done((s32[2,7680]{1,0:T(2,128)S(1)}, s32[2,7680]{1,0:T(2,128)}, u32[]{:S(2)}) %copy-start.2) | copy-done | bytes 61464
  2.8 0.0 copy-start.3
  2.8 0.8 %copy-done.3 = s32[2,7680]{1,0:T(2,128)S(1)} copy-done((s32[2,7680]{1,0:T(2,128)S(1)}, s32[2,7680]{1,0:T(2,128)}, u32[]{:S(2)}) %copy-start.3) | copy-done | bytes 61464
  3.6 0.0 copy-start.4
  3.6 0.8 %copy-done.4 = f32[2,7680]{1,0:T(2,128)S(1)} copy-done((f32[2,7680]{1,0:T(2,128)S(1)}, f32[2,7680]{1,0:T(2,128)}, u32[]{:S(2)}) %copy-start.4) | copy-done | bytes 61464
  4.4 0.0 copy-start.5
  4.4 0.8 %copy-done.5 = f32[2,7680]{1,0:T(2,128)S(1)} copy-done((f32[2,7680]{1,0:T(2,128)S(1)}, f32[2,7680]{1,0:T(2,128)}, u32[]{:S(2)}) %copy-start.5) | copy-done | bytes 61464
  5.3 36.7 %shard_map.64 = bf16[2,32,4096]{2,1,0:T(8,128)(2,1)S(1)} custom-call(bf16[2,2,256,256]{3,2,1,0:T(8,128)(2,1)S(1)} %copy-done, s32[2,7680]{1,0:T(2,128)S(1)} %copy-done.2, s32[2,7680]{1,0:T(2,128)S(1)} %copy-done.3, bf16[2,4,7680]{2,1,0:T(4,128)(2,1)S(1)} %copy-done.1, f32[2,7680]{1,0:T(2,128)S(1)} %copy-done.4, f32[2,7680]{1,0:T(2,128)S(1)} %copy-done.5), custom_call_target="tpu_custom_call" | custom-call | tf_op jit(solution)/shard_map/pallas_call | solution.py:341
  41.9 0.8 %copy.9 = bf16[2,1,1,32,4096]{4,3,2,1,0:T(8,128)(2,1)} copy(bf16[2,1,1,32,4096]{4,3,2,1,0:T(8,128)(2,1)S(1)} %bitcast.3) | data formatting | bytes 1048576
Async XLA Ops:
  0.0 1.0 %copy-start = (bf16[2,2,256,256]{3,2,1,0:T(8,128)(2,1)S(1)}, bf16[2,2,256,256]{3,2,1,0:T(8,128)(2,1)}, u32[]{:S(2)}) copy-start(bf16[2,2,256,256]{3,2,1,0:T(8,128)(2,1)} %images.1) | copy-start | bytes 1572868
  1.0 0.9 %copy-start.1 = (bf16[2,4,7680]{2,1,0:T(4,128)(2,1)S(1)}, bf16[2,4,7680]{2,1,0:T(4,128)(2,1)}, u32[]{:S(2)}) copy-start(bf16[2,4,7680]{2,1,0:T(4,128)(2,1)} %wts.1) | copy-start | bytes 368644
  1.9 0.8 %copy-start.2 = (s32[2,7680]{1,0:T(2,128)S(1)}, s32[2,7680]{1,0:T(2,128)}, u32[]{:S(2)}) copy-start(s32[2,7680]{1,0:T(2,128)} %idx.1) | copy-start | bytes 184324
  2.8 0.8 %copy-start.3 = (s32[2,7680]{1,0:T(2,128)S(1)}, s32[2,7680]{1,0:T(2,128)}, u32[]{:S(2)}) copy-start(s32[2,7680]{1,0:T(2,128)} %shf.1) | copy-start | bytes 184324
  3.6 0.8 %copy-start.4 = (f32[2,7680]{1,0:T(2,128)S(1)}, f32[2,7680]{1,0:T(2,128)}, u32[]{:S(2)}) copy-start(f32[2,7680]{1,0:T(2,128)} %base.1) | copy-start | bytes 184324
  4.4 0.8 %copy-start.5 = (f32[2,7680]{1,0:T(2,128)S(1)}, f32[2,7680]{1,0:T(2,128)}, u32[]{:S(2)}) copy-start(f32[2,7680]{1,0:T(2,128)} %slope.1) | copy-start | bytes 184324
where the time goes:
time: 43.1 us; the launch traced here: 42.7 us
  Pallas kernels  36.7 us (85%)
  local copies, waits for them, and re-layouts  6.05 us (14%)
    pallas_call x1, Pallas kernels, call(): pl.pallas_call(functools.partial(kernel, comm=comm, place=place), out_sha...  36.7 us
    unnamed x13, local copies, waits for them, and re-layouts  6.05 us

commit v1 on v0

v1 whole, which is shorter than its diff:
```python
import functools

import jax
import jax.numpy as jnp
from jax import lax
from jax.experimental import pallas as pl
from jax.experimental.pallas import tpu as pltpu
from jax.sharding import PartitionSpec as P

MESH = pl.DeviceIdType.MESH
BF16 = jnp.bfloat16
F32 = jnp.float32
CHIPS = 8
COLUMN = 8
STRIPS = 4
STRIP = 256
TILE = 32
HALO = 8
BLOCK = TILE + 2 * HALO
GROUP = 8
BEAMS = 256
LANES = 128
TAPS = 4
SHIFT = 2
TILES = (4, 8, 16, 32)
FIRST = (0, 4, 12, 28)
ROWS = (48, 40, 40, 32)
BASE = (-6, -4, -2, 0)
BAND_ROWS = 96
SLOTS = 4


def build_tables(z, q, idx, shf, wts, base, slope, band, cos_t, sin_t):
    origin_row = q * STRIP + z * TILE
    iota8 = lax.broadcasted_iota(jnp.int32, (8, LANES), 0)
    iota_k = lax.broadcasted_iota(jnp.int32, (BAND_ROWS, LANES), 0)

    def one(section, child, tile, origin, offset):
        cols = pl.ds(pl.multiple_of(tile * LANES, LANES), LANES)
        band[child, tile] = jnp.zeros((BEAMS, LANES), BF16)
        first = idx[child : child + 1, cols] - (origin + offset)
        weights = wts[child, :, cols].astype(F32)
        patch = jnp.zeros((BAND_ROWS, LANES), F32)
        for tap in range(TAPS):
            patch = jnp.where(iota_k == first + tap, weights[tap : tap + 1, :], patch)
        if not isinstance(offset, int):
            offset = pl.multiple_of(offset, 16)
        band[child, tile, pl.ds(offset, BAND_ROWS), :] = patch.astype(BF16)
        rate = slope[child : child + 1, cols]
        rows = (iota8 + (origin_row + BASE[section])).astype(F32)
        theta = base[child : child + 1, cols] + rate * rows
        c, s = jnp.cos(theta), jnp.sin(theta)
        turn = jnp.broadcast_to(rate * 8.0, (8, LANES))
        c8, s8 = jnp.cos(turn), jnp.sin(turn)
        for step in range(ROWS[section] // 8):
            cos_t[child, tile, step * 8 : step * 8 + 8, :] = c
            sin_t[child, tile, step * 8 : step * 8 + 8, :] = s
            c, s = c * c8 - s * s8, s * c8 + c * s8

    for child in range(2):
        for tile in range(TILES[0]):
            one(0, child, tile, 0, (0, 48, 112, 160)[tile])
    for section in range(1, 4):
        tiles = TILES[section]

        def body(tile, carry, section=section, tiles=tiles):
            block = (tile + 1) // 2
            side = (tile + 1) % 2
            for child in range(2):
                one(section, child, FIRST[section] + tile, LANES * (block - 1), 48 + 64 * side)
            return carry

        lax.fori_loop(0, tiles, body, 0)


def masks_of(shf, tile):
    found = []
    for child in range(2):
        cols = pl.ds(pl.multiple_of(tile * LANES, LANES), LANES)
        row = jnp.broadcast_to(shf[child : child + 1, cols], (16, LANES))
        found.append({o: row == o for o in (-2, -1, 1, 2)})
    return found


def merged_rows(v, slot, masks, cos_t, sin_t, tile, row, count):
    moved = []
    for child in range(2):
        for plane in range(2):
            at = row + SHIFT
            u = v[(*slot, child, plane, slice(at, at + count), slice(None))]
            for o in (-2, -1, 1, 2):
                other = v[(*slot, child, plane, slice(at + o, at + o + count), slice(None))]
                u = jnp.where(masks[child][o][:count], other, u)
            moved.append(u)
    rows = slice(row, row + count)
    c0, s0 = cos_t[0, tile, rows, :], sin_t[0, tile, rows, :]
    c1, s1 = cos_t[1, tile, rows, :], sin_t[1, tile, rows, :]
    real = (c0 * moved[0] - s0 * moved[1]) + (c1 * moved[2] - s1 * moved[3])
    imag = (s0 * moved[0] + c0 * moved[1]) + (s1 * moved[2] + c1 * moved[3])
    return real, imag


def combine(section, row0, v, slot, masks, cos_t, sin_t, tile, store):
    rows = ROWS[section]
    for row in range(0, rows, 16):
        count = min(16, rows - row)
        parts = merged_rows(v, slot, masks, cos_t, sin_t, tile, row, count)
        if section < 3 and row != 16:
            bins = lax.broadcasted_iota(jnp.int32, (count, LANES), 0) + (row0 + row + BASE[section])
            inside = (bins >= 0) & (bins < STRIPS * STRIP)
            parts = [jnp.where(inside, part, 0.0) for part in parts]
        if count < 16:
            rest = jnp.zeros((16 - count, LANES), F32)
            parts = [jnp.concatenate([part, rest], axis=0) for part in parts]
        for plane in range(2):
            store(plane, row, parts[plane].astype(BF16))


def section_zero(image, row0, recv, shf, band, cos_t, sin_t, v, out):
    for child in range(2):
        lhs = recv[image, :, child, 1 : 1 + BLOCK // GROUP].reshape(2 * BLOCK, BEAMS)
        rhs = jnp.concatenate([band[child, t] for t in range(4)], axis=1)
        product = jnp.dot(lhs, rhs, preferred_element_type=F32)
        for plane in range(2):
            for t in range(4):
                v[0, t, child, plane, 0:BLOCK, :] = product[
                    plane * BLOCK : (plane + 1) * BLOCK, t * LANES : (t + 1) * LANES
                ]
    for t in range(4):

        def store(plane, row, value, t=t):
            out[plane, image, row : row + 16, (t + 1) * LANES : (t + 2) * LANES] = value
            if t == 3:
                out[plane, image, row : row + 16, 0:LANES] = value

        combine(0, row0, v, (0, t), masks_of(shf, t), cos_t, sin_t, t, store)


def section_later(section, row0, source, shf, band, cos_t, sin_t, v, out):
    images = 8 >> section
    tiles = TILES[section]

    def tiles_of(block):
        return (lax.rem(2 * block + tiles - 1, tiles), 2 * block)

    def multiply(slot, block):
        window = pl.ds(pl.multiple_of(block * LANES, LANES), BEAMS)
        here = tiles_of(block)
        for child in range(2):
            lhs = source[:, child * images : (child + 1) * images, :, window]
            lhs = lhs.reshape(2 * images * BLOCK, BEAMS)
            rhs = jnp.concatenate([band[child, FIRST[section] + t] for t in here], axis=1)
            product = jnp.dot(lhs, rhs, preferred_element_type=F32)
            for plane in range(2):
                for image in range(images):
                    at = (plane * images + image) * BLOCK
                    for side in range(2):
                        v[slot, 2 * image + side, child, plane, 0:BLOCK, :] = product[
                            at : at + BLOCK, side * LANES : (side + 1) * LANES
                        ]

    def finish(slot, block):
        for side, t in enumerate(tiles_of(block)):
            tile = FIRST[section] + t
            masks = masks_of(shf, tile)
            for image in range(images):

                def store(plane, row, value, side=side, t=t, image=image):
                    if section == 3:
                        cols = pl.ds(pl.multiple_of(t * LANES, LANES), LANES)
                        out[plane, row : row + 16, cols] = value
                        return
                    cols = pl.ds(pl.multiple_of((t + 1) * LANES, LANES), LANES)
                    out[plane, image, row : row + 16, cols] = value
                    if side == 0 and isinstance(block, int) and block == 0:
                        out[plane, image, row : row + 16, 0:LANES] = value

                combine(section, row0, v, (slot, 2 * image + side), masks, cos_t, sin_t, tile, store)

    def step(first):
        multiply(0, first)
        for slot in range(1, SLOTS):
            multiply(slot, first + slot)
            finish(slot - 1, first + slot - 1)
        finish(SLOTS - 1, first + SLOTS - 1)

    def body(turn, carry):
        step(turn * SLOTS)
        return carry

    lax.fori_loop(0, tiles // 2 // SLOTS, body, 0)
    if section < 3:
        out[:, :, :, 0:LANES] = out[:, :, :, tiles * LANES : (tiles + 1) * LANES]


def kernel(
    images, idx_h, shf_h, wts_h, base_h, slope_h, final,
    recv, idx, shf, wts, base, slope, band, cos_t, sin_t, s1, s2, s3, v,
    local_sem, table_sem, send_sem, recv_sem, hsend_sem, hrecv_sem, comm=True, place=None,
):
    if comm:
        sub, q = lax.axis_index("sub"), lax.axis_index("rng")
        z, lane = sub // COLUMN, sub % COLUMN
    else:
        z, q = jnp.int32(place[0]), jnp.int32(place[1])

    def device(zz, qq):
        return (zz * COLUMN + lane, qq)

    if comm:
        barrier = pltpu.get_barrier_semaphore()
        for step in range(1, CHIPS):
            pl.semaphore_signal(
                barrier, inc=1, device_id=device((z + step) % CHIPS, q), device_id_type=MESH
            )

        @pl.when((z == 0) & (q > 0))
        def _():
            for other in range(CHIPS):
                pl.semaphore_signal(
                    barrier, inc=1, device_id=device(other, q - 1), device_id_type=MESH
                )

        @pl.when((z == CHIPS - 1) & (q < STRIPS - 1))
        def _():
            for other in range(CHIPS):
                pl.semaphore_signal(
                    barrier, inc=1, device_id=device(other, q + 1), device_id_type=MESH
                )

    fetches = [
        pltpu.make_async_copy(src, dst, table_sem.at[i])
        for i, (src, dst) in enumerate(
            ((idx_h, idx), (shf_h, shf), (wts_h, wts), (base_h, base), (slope_h, slope))
        )
    ]
    for fetch in fetches:
        fetch.start()

    groups = BLOCK // GROUP

    def spans(to):
        wanted = to * (TILE // GROUP) - 1
        begin = jnp.clip(wanted, 0, STRIP // GROUP - groups)
        return pl.ds(begin, groups), pl.ds(1 + begin - wanted, groups)

    if comm:
        src, dst = spans(z)
        own = pltpu.make_async_copy(
            images.at[:, :, src], recv.at[z, :, :, dst], local_sem
        )
        own.start()
        peers = CHIPS - 1 + (q > 0).astype(jnp.int32) + (q < STRIPS - 1).astype(jnp.int32)
        pl.semaphore_wait(barrier, peers)

        def block_copy(step):
            to = (z + step) % CHIPS
            src, dst = spans(to)
            return pltpu.make_async_remote_copy(
                src_ref=images.at[:, :, src],
                dst_ref=recv.at[z, :, :, dst],
                send_sem=send_sem.at[step],
                recv_sem=recv_sem.at[step],
                device_id=device(to, q),
                device_id_type=MESH,
            )

        def halo_copy(side):
            src, dst = ((STRIP // GROUP - 1, 1), (0, groups))[side]
            return pltpu.make_async_remote_copy(
                src_ref=images.at[:, :, src],
                dst_ref=recv.at[z, :, :, dst],
                send_sem=hsend_sem.at[side],
                recv_sem=hrecv_sem.at[z],
                device_id=device(0, q + 1) if side == 0 else device(CHIPS - 1, q - 1),
                device_id_type=MESH,
            )

        for step in (1, 7, 2, 6, 3, 5, 4):
            block_copy(step).start()

        @pl.when(q < STRIPS - 1)
        def _():
            halo_copy(0).start()

        @pl.when(q > 0)
        def _():
            halo_copy(1).start()

        @pl.when((z == 0) & (q == 0))
        def _():
            recv[:, :, :, 1] = jnp.zeros((CHIPS, 2, 2, GROUP, BEAMS), BF16)

        @pl.when((z == CHIPS - 1) & (q == STRIPS - 1))
        def _():
            recv[:, :, :, groups] = jnp.zeros((CHIPS, 2, 2, GROUP, BEAMS), BF16)
    else:
        own = pltpu.make_async_copy(images, recv.at[:, :, :, pl.ds(1, groups)], local_sem)
        own.start()

    for fetch in fetches:
        fetch.wait()
    build_tables(z, q, idx, shf, wts, base, slope, band, cos_t, sin_t)
    own.wait()
    row0 = q * STRIP + z * TILE

    def arrival(turn, carry):
        step = jnp.where(turn % 2 == 1, (turn + 1) // 2, (CHIPS - turn // 2) % CHIPS)
        image = (z + CHIPS - step) % CHIPS
        if comm:

            @pl.when(turn > 0)
            def _():
                src, dst = spans(z)
                pltpu.make_async_remote_copy(
                    src_ref=images.at[:, :, src],
                    dst_ref=recv.at[image, :, :, dst],
                    send_sem=send_sem.at[step],
                    recv_sem=recv_sem.at[step],
                    device_id=device(image, q),
                    device_id_type=MESH,
                ).wait_recv()

            def halo_wait(at):
                pltpu.make_async_remote_copy(
                    src_ref=images.at[:, :, 0],
                    dst_ref=recv.at[image, :, :, at],
                    send_sem=hsend_sem.at[0],
                    recv_sem=hrecv_sem.at[image],
                    device_id=device(image, q),
                    device_id_type=MESH,
                ).wait_recv()

            @pl.when((z == 0) & (q > 0))
            def _():
                halo_wait(1)

            @pl.when((z == CHIPS - 1) & (q < STRIPS - 1))
            def _():
                halo_wait(groups)

        section_zero(image, row0, recv, shf, band, cos_t, sin_t, v, s1)
        return carry

    lax.fori_loop(0, CHIPS, arrival, 0)
    section_later(1, row0, s1, shf, band, cos_t, sin_t, v, s2)
    section_later(2, row0, s2, shf, band, cos_t, sin_t, v, s3)
    section_later(3, row0, s3, shf, band, cos_t, sin_t, v, final)

    if comm:
        for step in range(1, CHIPS):
            block_copy(step).wait_send()

        @pl.when(q < STRIPS - 1)
        def _():
            halo_copy(0).wait_send()

        @pl.when(q > 0)
        def _():
            halo_copy(1).wait_send()


def call(images, tables, comm=True, place=None):
    vmem = pl.BlockSpec(memory_space=pltpu.VMEM)
    hbm = pl.BlockSpec(memory_space=pltpu.HBM)
    dma = pltpu.SemaphoreType.DMA
    tiles = sum(TILES)
    params = dict(vmem_limit_bytes=62 * 2**20, has_side_effects=True)
    if comm:
        params["collective_id"] = 0
    return pl.pallas_call(
        functools.partial(kernel, comm=comm, place=place),
        out_shape=jax.ShapeDtypeStruct((2, TILE, 4096), BF16),
        in_specs=[hbm] * 6,
        out_specs=vmem,
        scratch_shapes=[
            pltpu.VMEM((CHIPS, 2, 2, BLOCK // GROUP + 2, GROUP, BEAMS), BF16),
            *[pltpu.VMEM(table.shape, table.dtype) for table in tables],
            pltpu.VMEM((2, tiles, BEAMS, LANES), BF16),
            pltpu.VMEM((2, tiles, BLOCK, LANES), F32),
            pltpu.VMEM((2, tiles, BLOCK, LANES), F32),
            pltpu.VMEM((2, 8, BLOCK, 512 + LANES), BF16),
            pltpu.VMEM((2, 4, BLOCK, 1024 + LANES), BF16),
            pltpu.VMEM((2, 2, BLOCK, 2048 + LANES), BF16),
            pltpu.VMEM((SLOTS, 8, 2, 2, BLOCK + GROUP, LANES), F32),
            dma,
            dma((len(tables),)),
            dma((CHIPS,)),
            dma((CHIPS,)),
            dma((2,)),
            dma((CHIPS,)),
        ],
        compiler_params=pltpu.CompilerParams(**params),
    )(images, *tables)


def local(images, *tables):
    grouped = images.reshape(2, 2, STRIP // GROUP, GROUP, BEAMS)
    return call(grouped, tables).reshape(2, 1, 1, TILE, 4096)


def solution(mesh):
    in_specs = (P(None, "sub", "rng", None), P(), P(), P(), P(), P())
    out_specs = P(None, "sub", "rng", None, None)
    return jax.shard_map(local, mesh=mesh, in_specs=in_specs, out_specs=out_specs, check_vma=False)
```

time: 43.1 us -> 37.8 us (0.88)
  local copies, waits for them, and re-layouts: 6.05 us -> 1.87 us
  Pallas kernels: 36.7 us -> 35.8 us
    unnamed x13 -> x1, local copies, waits for them, and re-layouts: 6.05 us -> 1.87 us
    pallas_call x1, Pallas kernels: 36.7 us -> 35.8 us  [call(): pl.pallas_call(functools.partial(kernel, comm=comm, place=place), out_sha...]
where the time goes in v1:
time: 37.8 us; the launch traced here: 37.7 us
  Pallas kernels  35.8 us (95%)
  local copies, waits for them, and re-layouts  1.87 us (5%)
    pallas_call x1, Pallas kernels, call(): pl.pallas_call(functools.partial(kernel, comm=comm, place=place), out_sha...  35.8 us
    unnamed x1, local copies, waits for them, and re-layouts  1.87 us

profile of v1, /device:TPU:1, one launch (start us, length us, event | category | flops | bytes accessed | tf_op | source)
XLA Modules:
  0.0 37.7 jit_solution(11059387468121614530)
XLA Ops:
  0.0 35.8 %shard_map.64 = bf16[2,32,4096]{2,1,0:T(8,128)(2,1)} custom-call(bf16[2,2,32,8,256]{4,3,2,1,0:T(8,128)(2,1)} %bitcast.5, s32[2,7680]{1,0:T(2,128)} %idx_h.1, s32[2,7680]{1,0:T(2,128)} %shf_h.1, bf16[2,4,7680]{2,1,0:T(4,128)(2,1)} %wts_h.1, f32[2,7680]{1,0:T(2,128)} %base_h.1, f32[2,7680]{1,0:T(2,128)} %slope_h.1), custom_call_target="tpu_custom_call" | custom-call | tf_op jit(solution)/shard_map/pallas_call | solution.py:371
  35.8 1.9 %copy.9 = bf16[2,1,1,32,4096]{4,3,2,1,0:T(8,128)(2,1)} copy(bf16[2,1,1,32,4096]{4,3,2,1,0:T(8,128)(2,1)} %bitcast.4) | data formatting | bytes 1048576

commit v2 on v1

--- a/solution.py
+++ b/solution.py
@@ -27,10 +27,11 @@
 ROWS = (48, 40, 40, 32)
 BASE = (-6, -4, -2, 0)
 BAND_ROWS = 96
+STEPS = (1, 7, 2, 6, 3, 5)
 SLOTS = 4
 
 
-def build_tables(z, q, idx, shf, wts, base, slope, band, cos_t, sin_t):
+def build_tables(z, q, idx, shf, wts, base, slope, band, cos_t, sin_t, sections):
     origin_row = q * STRIP + z * TILE
     iota8 = lax.broadcasted_iota(jnp.int32, (8, LANES), 0)
     iota_k = lax.broadcasted_iota(jnp.int32, (BAND_ROWS, LANES), 0)
@@ -57,10 +58,12 @@
             sin_t[child, tile, step * 8 : step * 8 + 8, :] = s
             c, s = c * c8 - s * s8, s * c8 + c * s8
 
-    for child in range(2):
+    for child in range(2 if 0 in sections else 0):
         for tile in range(TILES[0]):
             one(0, child, tile, 0, (0, 48, 112, 160)[tile])
-    for section in range(1, 4):
+    for section in sections:
+        if section == 0:
+            continue
         tiles = TILES[section]
 
         def body(tile, carry, section=section, tiles=tiles):
@@ -118,7 +121,7 @@
 
 def section_zero(image, row0, recv, shf, band, cos_t, sin_t, v, out):
     for child in range(2):
-        lhs = recv[image, :, child, 1 : 1 + BLOCK // GROUP].reshape(2 * BLOCK, BEAMS)
+        lhs = recv[image, :, child].reshape(2 * BLOCK, BEAMS)
         rhs = jnp.concatenate([band[child, t] for t in range(4)], axis=1)
         product = jnp.dot(lhs, rhs, preferred_element_type=F32)
         for plane in range(2):
@@ -195,8 +198,8 @@
 
 def kernel(
     images, idx_h, shf_h, wts_h, base_h, slope_h, final,
-    recv, idx, shf, wts, base, slope, band, cos_t, sin_t, s1, s2, s3, v,
-    local_sem, table_sem, send_sem, recv_sem, hsend_sem, hrecv_sem, comm=True, place=None,
+    recv, relay, idx, shf, wts, base, slope, band, cos_t, sin_t, s1, s2, s3, v,
+    local_sem, table_sem, send_sem, recv_sem, relay_sem, forward_sem, margin_sem, comm=True, place=None,
 ):
     if comm:
         sub, q = lax.axis_index("sub"), lax.axis_index("rng")
@@ -206,6 +209,15 @@
 
     def device(zz, qq):
         return (zz * COLUMN + lane, qq)
+
+    groups = TILE // GROUP
+    has_next = (z < CHIPS - 1) | (q < STRIPS - 1)
+    has_previous = (z > 0) | (q > 0)
+
+    def beside(side):
+        if side == 0:
+            return device((z + 1) % CHIPS, q + (z == CHIPS - 1).astype(jnp.int32))
+        return device((z + CHIPS - 1) % CHIPS, q - (z == 0).astype(jnp.int32))
 
     if comm:
         barrier = pltpu.get_barrier_semaphore()
@@ -213,20 +225,13 @@
             pl.semaphore_signal(
                 barrier, inc=1, device_id=device((z + step) % CHIPS, q), device_id_type=MESH
             )
-
-        @pl.when((z == 0) & (q > 0))
-        def _():
-            for other in range(CHIPS):
-                pl.semaphore_signal(
-                    barrier, inc=1, device_id=device(other, q - 1), device_id_type=MESH
-                )
-
-        @pl.when((z == CHIPS - 1) & (q < STRIPS - 1))
-        def _():
-            for other in range(CHIPS):
-                pl.semaphore_signal(
-                    barrier, inc=1, device_id=device(other, q + 1), device_id_type=MESH
-                )
+        leaves_up = (z == CHIPS - 1) & (q < STRIPS - 1)
+        leaves_down = (z == 0) & (q > 0)
+        for side, leaves in enumerate((leaves_up, leaves_down)):
+
+            @pl.when(leaves)
+            def _(side=side):
+                pl.semaphore_signal(barrier, inc=1, device_id=beside(side), device_id_type=MESH)
 
     fetches = [
         pltpu.make_async_copy(src, dst, table_sem.at[i])
@@ -237,107 +242,115 @@
     for fetch in fetches:
         fetch.start()
 
-    groups = BLOCK // GROUP
-
-    def spans(to):
-        wanted = to * (TILE // GROUP) - 1
-        begin = jnp.clip(wanted, 0, STRIP // GROUP - groups)
-        return pl.ds(begin, groups), pl.ds(1 + begin - wanted, groups)
-
-    if comm:
-        src, dst = spans(z)
+    main = pl.ds(1, groups)
+
+    def of_tile(to, first=0, count=groups):
+        return pl.ds(to * groups + first, count)
+
+    if comm:
         own = pltpu.make_async_copy(
-            images.at[:, :, src], recv.at[z, :, :, dst], local_sem
+            images.at[:, :, of_tile(z)], recv.at[z, :, :, main], local_sem
         )
         own.start()
-        peers = CHIPS - 1 + (q > 0).astype(jnp.int32) + (q < STRIPS - 1).astype(jnp.int32)
+        peers = CHIPS - 1 + leaves_up.astype(jnp.int32) + leaves_down.astype(jnp.int32)
         pl.semaphore_wait(barrier, peers)
 
         def block_copy(step):
             to = (z + step) % CHIPS
-            src, dst = spans(to)
             return pltpu.make_async_remote_copy(
-                src_ref=images.at[:, :, src],
-                dst_ref=recv.at[z, :, :, dst],
+                src_ref=images.at[:, :, of_tile(to)],
+                dst_ref=recv.at[z, :, :, main],
                 send_sem=send_sem.at[step],
                 recv_sem=recv_sem.at[step],
                 device_id=device(to, q),
                 device_id_type=MESH,
             )
 
-        def halo_copy(side):
-            src, dst = ((STRIP // GROUP - 1, 1), (0, groups))[side]
+        def relay_copy(way):
             return pltpu.make_async_remote_copy(
-                src_ref=images.at[:, :, src],
-                dst_ref=recv.at[z, :, :, dst],
-                send_sem=hsend_sem.at[side],
-                recv_sem=hrecv_sem.at[z],
-                device_id=device(0, q + 1) if side == 0 else device(CHIPS - 1, q - 1),
+                src_ref=images.at[:, :, of_tile((z + 4) % CHIPS, 2 * way, 2)],
+                dst_ref=relay.at[way],
+                send_sem=relay_sem.at[0, way],
+                recv_sem=relay_sem.at[1, way],
+                device_id=device((z + (2, 6)[way]) % CHIPS, q),
                 device_id_type=MESH,
             )
 
-        for step in (1, 7, 2, 6, 3, 5, 4):
+        def forward_copy(way):
+            return pltpu.make_async_remote_copy(
+                src_ref=relay.at[way],
+                dst_ref=recv.at[(z + (6, 2)[way]) % CHIPS, :, :, pl.ds(1 + 2 * way, 2)],
+                send_sem=forward_sem.at[0, way],
+                recv_sem=forward_sem.at[1, way],
+                device_id=device((z + (2, 6)[way]) % CHIPS, q),
+                device_id_type=MESH,
+            )
+
+        def margin_copy(side, image):
+            return pltpu.make_async_remote_copy(
+                src_ref=recv.at[image, :, :, (groups, 1)[side]],
+                dst_ref=recv.at[image, :, :, (0, groups + 1)[side]],
+                send_sem=margin_sem.at[0, side, image],
+                recv_sem=margin_sem.at[1, side, image],
+                device_id=beside(side),
+                device_id_type=MESH,
+            )
+
+        for way in range(2):
+            relay_copy(way).start()
+        for step in STEPS:
             block_copy(step).start()
 
-        @pl.when(q < STRIPS - 1)
+        @pl.when(jnp.logical_not(has_previous))
         def _():
-            halo_copy(0).start()
-
-        @pl.when(q > 0)
+            recv[:, :, :, 0] = jnp.zeros((CHIPS, 2, 2, GROUP, BEAMS), BF16)
+
+        @pl.when(jnp.logical_not(has_next))
         def _():
-            halo_copy(1).start()
-
-        @pl.when((z == 0) & (q == 0))
-        def _():
-            recv[:, :, :, 1] = jnp.zeros((CHIPS, 2, 2, GROUP, BEAMS), BF16)
-
-        @pl.when((z == CHIPS - 1) & (q == STRIPS - 1))
-        def _():
-            recv[:, :, :, groups] = jnp.zeros((CHIPS, 2, 2, GROUP, BEAMS), BF16)
+            recv[:, :, :, groups + 1] = jnp.zeros((CHIPS, 2, 2, GROUP, BEAMS), BF16)
     else:
-        own = pltpu.make_async_copy(images, recv.at[:, :, :, pl.ds(1, groups)], local_sem)
+        own = pltpu.make_async_copy(images, recv, local_sem)
         own.start()
 
     for fetch in fetches:
         fetch.wait()
-    build_tables(z, q, idx, shf, wts, base, slope, band, cos_t, sin_t)
+    tables = (z, q, idx, shf, wts, base, slope, band, cos_t, sin_t)
+    build_tables(*tables, sections=(0, 1, 2))
+    if comm:
+        for way in range(2):
+            relay_copy(way).wait_recv()
+            forward_copy(way).start()
+    build_tables(*tables, sections=(3,))
     own.wait()
     row0 = q * STRIP + z * TILE
 
+    if comm:
+
+        def spread(image):
+            for side, there in enumerate((has_next, has_previous)):
+
+                @pl.when(there)
+                def _(side=side):
+                    margin_copy(side, image).start()
+
+        spread(z)
+        for step in STEPS:
+            block_copy(step).wait_recv()
+            spread((z + CHIPS - step) % CHIPS)
+        for way in range(2):
+            forward_copy(way).wait_recv()
+        spread((z + 4) % CHIPS)
+
     def arrival(turn, carry):
-        step = jnp.where(turn % 2 == 1, (turn + 1) // 2, (CHIPS - turn // 2) % CHIPS)
-        image = (z + CHIPS - step) % CHIPS
+        image = (z + turn) % CHIPS
         if comm:
-
-            @pl.when(turn > 0)
+            @pl.when(has_previous)
             def _():
-                src, dst = spans(z)
-                pltpu.make_async_remote_copy(
-                    src_ref=images.at[:, :, src],
-                    dst_ref=recv.at[image, :, :, dst],
-                    send_sem=send_sem.at[step],
-                    recv_sem=recv_sem.at[step],
-                    device_id=device(image, q),
-                    device_id_type=MESH,
-                ).wait_recv()
-
-            def halo_wait(at):
-                pltpu.make_async_remote_copy(
-                    src_ref=images.at[:, :, 0],
-                    dst_ref=recv.at[image, :, :, at],
-                    send_sem=hsend_sem.at[0],
-                    recv_sem=hrecv_sem.at[image],
-                    device_id=device(image, q),
-                    device_id_type=MESH,
-                ).wait_recv()
-
-            @pl.when((z == 0) & (q > 0))
+                margin_copy(0, image).wait_recv()
+
+            @pl.when(has_next)
             def _():
-                halo_wait(1)
-
-            @pl.when((z == CHIPS - 1) & (q < STRIPS - 1))
-            def _():
-                halo_wait(groups)
+                margin_copy(1, image).wait_recv()
 
         section_zero(image, row0, recv, shf, band, cos_t, sin_t, v, s1)
         return carry
@@ -348,16 +361,17 @@
     section_later(3, row0, s3, shf, band, cos_t, sin_t, v, final)
 
     if comm:
-        for step in range(1, CHIPS):
+        for way in range(2):
+            relay_copy(way).wait_send()
+            forward_copy(way).wait_send()
+        for step in STEPS:
             block_copy(step).wait_send()
-
-        @pl.when(q < STRIPS - 1)
-        def _():
-            halo_copy(0).wait_send()
-
-        @pl.when(q > 0)
-        def _():
-            halo_copy(1).wait_send()
+        for side, there in enumerate((has_next, has_previous)):
+
+            @pl.when(there)
+            def _(side=side):
+                for image in range(CHIPS):
+                    margin_copy(side, image).wait_send()
 
 
 def call(images, tables, comm=True, place=None):
@@ -374,7 +388,8 @@
         in_specs=[hbm] * 6,
         out_specs=vmem,
         scratch_shapes=[
-            pltpu.VMEM((CHIPS, 2, 2, BLOCK // GROUP + 2, GROUP, BEAMS), BF16),
+            pltpu.VMEM((CHIPS, 2, 2, BLOCK // GROUP, GROUP, BEAMS), BF16),
+            pltpu.VMEM((2, 2, 2, 2, GROUP, BEAMS), BF16),
             *[pltpu.VMEM(table.shape, table.dtype) for table in tables],
             pltpu.VMEM((2, tiles, BEAMS, LANES), BF16),
             pltpu.VMEM((2, tiles, BLOCK, LANES), F32),
@@ -387,8 +402,9 @@
             dma((len(tables),)),
             dma((CHIPS,)),
             dma((CHIPS,)),
-            dma((2,)),
-            dma((CHIPS,)),
+            dma((2, 2)),
+            dma((2, 2)),
+            dma((2, 2, CHIPS)),
         ],
         compiler_params=pltpu.CompilerParams(**params),
     )(images, *tables)

time: 37.8 us -> 36 us (0.952)
  Pallas kernels: 35.8 us -> 34 us
    pallas_call x1, Pallas kernels: 35.8 us -> 34 us  [call(): pl.pallas_call(functools.partial(kernel, comm=comm, place=place), out_sha...]
where the time goes in v2:
time: 36 us; the launch traced here: 35.9 us
  Pallas kernels  34 us (94%)
  local copies, waits for them, and re-layouts  1.87 us (5%)
    pallas_call x1, Pallas kernels, call(): pl.pallas_call(functools.partial(kernel, comm=comm, place=place), out_sha...  34 us
    unnamed x1, local copies, waits for them, and re-layouts  1.87 us

profile of v2, /device:TPU:1, one launch (start us, length us, event | category | flops | bytes accessed | tf_op | source)
XLA Modules:
  0.0 35.9 jit_solution(13454814320197955855)
XLA Ops:
  0.0 34.0 %shard_map.64 = bf16[2,32,4096]{2,1,0:T(8,128)(2,1)} custom-call(bf16[2,2,32,8,256]{4,3,2,1,0:T(8,128)(2,1)} %bitcast.5, s32[2,7680]{1,0:T(2,128)} %idx_h.1, s32[2,7680]{1,0:T(2,128)} %shf_h.1, bf16[2,4,7680]{2,1,0:T(4,128)(2,1)} %wts_h.1, f32[2,7680]{1,0:T(2,128)} %base_h.1, f32[2,7680]{1,0:T(2,128)} %slope_h.1), custom_call_target="tpu_custom_call" | custom-call | tf_op jit(solution)/shard_map/pallas_call | solution.py:385
  34.0 1.9 %copy.9 = bf16[2,1,1,32,4096]{4,3,2,1,0:T(8,128)(2,1)} copy(bf16[2,1,1,32,4096]{4,3,2,1,0:T(8,128)(2,1)} %bitcast.4) | data formatting | bytes 1048576

commit v3 on v2

--- a/solution.py
+++ b/solution.py
@@ -27,7 +27,7 @@
 ROWS = (48, 40, 40, 32)
 BASE = (-6, -4, -2, 0)
 BAND_ROWS = 96
-STEPS = (1, 7, 2, 6, 3, 5)
+STEPS = (3, 5, 2, 6, 1, 7)
 SLOTS = 4
 
 
@@ -85,63 +85,88 @@
     return found
 
 
-def merged_rows(v, slot, masks, cos_t, sin_t, tile, row, count):
-    moved = []
-    for child in range(2):
-        for plane in range(2):
-            at = row + SHIFT
-            u = v[(*slot, child, plane, slice(at, at + count), slice(None))]
-            for o in (-2, -1, 1, 2):
-                other = v[(*slot, child, plane, slice(at + o, at + o + count), slice(None))]
-                u = jnp.where(masks[child][o][:count], other, u)
-            moved.append(u)
-    rows = slice(row, row + count)
-    c0, s0 = cos_t[0, tile, rows, :], sin_t[0, tile, rows, :]
-    c1, s1 = cos_t[1, tile, rows, :], sin_t[1, tile, rows, :]
-    real = (c0 * moved[0] - s0 * moved[1]) + (c1 * moved[2] - s1 * moved[3])
-    imag = (s0 * moved[0] + c0 * moved[1]) + (s1 * moved[2] + c1 * moved[3])
-    return real, imag
-
-
-def combine(section, row0, v, slot, masks, cos_t, sin_t, tile, store):
-    rows = ROWS[section]
-    for row in range(0, rows, 16):
-        count = min(16, rows - row)
-        parts = merged_rows(v, slot, masks, cos_t, sin_t, tile, row, count)
-        if section < 3 and row != 16:
-            bins = lax.broadcasted_iota(jnp.int32, (count, LANES), 0) + (row0 + row + BASE[section])
+def pieces_of(section, part):
+    if part == 1:
+        low, high = (0, 24) if section == 3 else (32, 56)
+        return (
+            (2, 0, 8, ((low, 0, 8, 8),)),
+            (22, 36 - 4 * section, 8, ((high, 0, 8, 8),)),
+        )
+    if section == 3:
+        return ((2, 8, 16, ((8, 0, 8, 8), (16, 8, 8, 8))),)
+    start = (2, 8, 16, ((0, 0, 16, 16), (40, 0, 8, 8)))
+    if section == 0:
+        return (start, (18, 24, 16, ((16, 0, 16, 16),)), (22, 28, 8, ((48, 0, 8, 8),)))
+    if section == 1:
+        return (start, (18, 24, 8, ((16, 0, 8, 16), (48, 0, 8, 8))))
+    return (start, (18, 24, 8, ((16, 0, 8, 16),)), (14, 20, 8, ((48, 0, 8, 8),)))
+
+
+def combine(section, part, row0, v, slot, masks, cos_t, sin_t, tile, store):
+    for at, phase, count, places in pieces_of(section, part):
+        moved = []
+        for child in range(2):
+            for plane in range(2):
+                u = v[(*slot, child, plane, slice(at, at + count), slice(None))]
+                for o in (-2, -1, 1, 2):
+                    other = v[(*slot, child, plane, slice(at + o, at + o + count), slice(None))]
+                    u = jnp.where(masks[child][o][:count], other, u)
+                moved.append(u)
+        rows = slice(phase, phase + count)
+        c0, s0 = cos_t[0, tile, rows, :], sin_t[0, tile, rows, :]
+        c1, s1 = cos_t[1, tile, rows, :], sin_t[1, tile, rows, :]
+        parts = [
+            (c0 * moved[0] - s0 * moved[1]) + (c1 * moved[2] - s1 * moved[3]),
+            (s0 * moved[0] + c0 * moved[1]) + (s1 * moved[2] + c1 * moved[3]),
+        ]
+        if part == 1 and section < 3:
+            bins = lax.broadcasted_iota(jnp.int32, (count, LANES), 0)
+            bins = bins + (row0 + phase + BASE[section])
             inside = (bins >= 0) & (bins < STRIPS * STRIP)
-            parts = [jnp.where(inside, part, 0.0) for part in parts]
-        if count < 16:
-            rest = jnp.zeros((16 - count, LANES), F32)
-            parts = [jnp.concatenate([part, rest], axis=0) for part in parts]
-        for plane in range(2):
-            store(plane, row, parts[plane].astype(BF16))
-
-
-def section_zero(image, row0, recv, shf, band, cos_t, sin_t, v, out):
-    for child in range(2):
-        lhs = recv[image, :, child].reshape(2 * BLOCK, BEAMS)
-        rhs = jnp.concatenate([band[child, t] for t in range(4)], axis=1)
-        product = jnp.dot(lhs, rhs, preferred_element_type=F32)
-        for plane in range(2):
-            for t in range(4):
-                v[0, t, child, plane, 0:BLOCK, :] = product[
-                    plane * BLOCK : (plane + 1) * BLOCK, t * LANES : (t + 1) * LANES
-                ]
+            parts = [jnp.where(inside, value, 0.0) for value in parts]
+        for to, first, taken, written in places:
+            for plane in range(2):
+                value = parts[plane][first : first + taken]
+                if written > taken:
+                    rest = jnp.zeros((written - taken, LANES), F32)
+                    value = jnp.concatenate([value, rest], axis=0)
+                store(plane, slice(to, to + written), value.astype(BF16))
+
+
+def section_zero(images, part, row0, recv, shf, band, cos_t, sin_t, v, out):
+    def slot_of(k, t):
+        return (k // 2, (k % 2) * 4 + t)
+
+    for k, image in enumerate(images):
+        for child in range(2):
+            if part == 0:
+                lhs = recv[image, :, child, 1:5].reshape(2 * 32, BEAMS)
+            else:
+                ends = [recv[image, :, child, at : at + 2].reshape(2, 16, BEAMS) for at in (0, 4)]
+                lhs = jnp.concatenate(ends, axis=1).reshape(2 * 32, BEAMS)
+            rhs = jnp.concatenate([band[child, t] for t in range(4)], axis=1)
+            product = jnp.dot(lhs, rhs, preferred_element_type=F32)
+            for plane in range(2):
+                for t in range(4):
+                    v[(*slot_of(k, t), child, plane, slice(0, 32), slice(None))] = product[
+                        plane * 32 : (plane + 1) * 32, t * LANES : (t + 1) * LANES
+                    ]
     for t in range(4):
-
-        def store(plane, row, value, t=t):
-            out[plane, image, row : row + 16, (t + 1) * LANES : (t + 2) * LANES] = value
-            if t == 3:
-                out[plane, image, row : row + 16, 0:LANES] = value
-
-        combine(0, row0, v, (0, t), masks_of(shf, t), cos_t, sin_t, t, store)
-
-
-def section_later(section, row0, source, shf, band, cos_t, sin_t, v, out):
+        masks = masks_of(shf, t)
+        for k, image in enumerate(images):
+
+            def store(plane, rows, value, t=t, image=image):
+                out[plane, image, rows, (t + 1) * LANES : (t + 2) * LANES] = value
+                if t == 3:
+                    out[plane, image, rows, 0:LANES] = value
+
+            combine(0, part, row0, v, slot_of(k, t), masks, cos_t, sin_t, t, store)
+
+
+def section_later(section, part, row0, source, shf, band, cos_t, sin_t, v, out):
     images = 8 >> section
     tiles = TILES[section]
+    half = slice(part * 32, part * 32 + 32)
 
     def tiles_of(block):
         return (lax.rem(2 * block + tiles - 1, tiles), 2 * block)
@@ -150,16 +175,16 @@
         window = pl.ds(pl.multiple_of(block * LANES, LANES), BEAMS)
         here = tiles_of(block)
         for child in range(2):
-            lhs = source[:, child * images : (child + 1) * images, :, window]
-            lhs = lhs.reshape(2 * images * BLOCK, BEAMS)
+            lhs = source[:, child * images : (child + 1) * images, half, window]
+            lhs = lhs.reshape(2 * images * 32, BEAMS)
             rhs = jnp.concatenate([band[child, FIRST[section] + t] for t in here], axis=1)
             product = jnp.dot(lhs, rhs, preferred_element_type=F32)
             for plane in range(2):
                 for image in range(images):
-                    at = (plane * images + image) * BLOCK
+                    at = (plane * images + image) * 32
                     for side in range(2):
-                        v[slot, 2 * image + side, child, plane, 0:BLOCK, :] = product[
-                            at : at + BLOCK, side * LANES : (side + 1) * LANES
+                        v[slot, 2 * image + side, child, plane, 0:32, :] = product[
+                            at : at + 32, side * LANES : (side + 1) * LANES
                         ]
 
     def finish(slot, block):
@@ -168,32 +193,29 @@
             masks = masks_of(shf, tile)
             for image in range(images):
 
-                def store(plane, row, value, side=side, t=t, image=image):
+                def store(plane, rows, value, t=t, image=image):
                     if section == 3:
                         cols = pl.ds(pl.multiple_of(t * LANES, LANES), LANES)
-                        out[plane, row : row + 16, cols] = value
-                        return
-                    cols = pl.ds(pl.multiple_of((t + 1) * LANES, LANES), LANES)
-                    out[plane, image, row : row + 16, cols] = value
-                    if side == 0 and isinstance(block, int) and block == 0:
-                        out[plane, image, row : row + 16, 0:LANES] = value
-
-                combine(section, row0, v, (slot, 2 * image + side), masks, cos_t, sin_t, tile, store)
-
-    def step(first):
+                        out[plane, rows, cols] = value
+                    else:
+                        cols = pl.ds(pl.multiple_of((t + 1) * LANES, LANES), LANES)
+                        out[plane, image, rows, cols] = value
+
+                slots = (slot, 2 * image + side)
+                combine(section, part, row0, v, slots, masks, cos_t, sin_t, tile, store)
+
+    def body(turn, carry):
+        first = turn * SLOTS
         multiply(0, first)
         for slot in range(1, SLOTS):
             multiply(slot, first + slot)
             finish(slot - 1, first + slot - 1)
         finish(SLOTS - 1, first + SLOTS - 1)
-
-    def body(turn, carry):
-        step(turn * SLOTS)
         return carry
 
     lax.fori_loop(0, tiles // 2 // SLOTS, body, 0)
     if section < 3:
-        out[:, :, :, 0:LANES] = out[:, :, :, tiles * LANES : (tiles + 1) * LANES]
+        out[:, :, half, 0:LANES] = out[:, :, half, tiles * LANES : (tiles + 1) * LANES]
 
 
 def kernel(
@@ -324,26 +346,34 @@
     own.wait()
     row0 = q * STRIP + z * TILE
 
-    if comm:
-
-        def spread(image):
+    def arrival(turn, carry):
+        far = 3 - (turn - 1) // 2
+        step = jnp.where(turn % 2 == 1, far, CHIPS - far)
+        step = jnp.where(turn == 0, 0, jnp.where(turn == CHIPS - 1, 4, step))
+        image = (z + CHIPS - step) % CHIPS
+        if comm:
+
+            @pl.when((turn > 0) & (turn < CHIPS - 1))
+            def _():
+                block_copy(step).wait_recv()
+
+            @pl.when(turn == CHIPS - 1)
+            def _():
+                for way in range(2):
+                    forward_copy(way).wait_recv()
+
             for side, there in enumerate((has_next, has_previous)):
 
                 @pl.when(there)
                 def _(side=side):
                     margin_copy(side, image).start()
 
-        spread(z)
-        for step in STEPS:
-            block_copy(step).wait_recv()
-            spread((z + CHIPS - step) % CHIPS)
-        for way in range(2):
-            forward_copy(way).wait_recv()
-        spread((z + 4) % CHIPS)
-
-    def arrival(turn, carry):
-        image = (z + turn) % CHIPS
+        section_zero([image], 0, row0, recv, shf, band, cos_t, sin_t, v, s1)
+        return carry
+
+    def margins(image, carry):
         if comm:
+
             @pl.when(has_previous)
             def _():
                 margin_copy(0, image).wait_recv()
@@ -352,13 +382,23 @@
             def _():
                 margin_copy(1, image).wait_recv()
 
-        section_zero(image, row0, recv, shf, band, cos_t, sin_t, v, s1)
         return carry
 
-    lax.fori_loop(0, CHIPS, arrival, 0)
-    section_later(1, row0, s1, shf, band, cos_t, sin_t, v, s2)
-    section_later(2, row0, s2, shf, band, cos_t, sin_t, v, s3)
-    section_later(3, row0, s3, shf, band, cos_t, sin_t, v, final)
+    def outer(turn, carry):
+        images = [turn * 4 + k for k in range(4)]
+        section_zero(images, 1, row0, recv, shf, band, cos_t, sin_t, v, s1)
+        return carry
+
+    arrays = (s1, s2, s3, final)
+    for part in range(2):
+        if part == 0:
+            lax.fori_loop(0, CHIPS, arrival, 0)
+        else:
+            lax.fori_loop(0, CHIPS, margins, 0)
+            lax.fori_loop(0, CHIPS // 4, outer, 0)
+        for section in range(1, 4):
+            source, out = arrays[section - 1 : section + 1]
+            section_later(section, part, row0, source, shf, band, cos_t, sin_t, v, out)
 
     if comm:
         for way in range(2):
@@ -379,7 +419,7 @@
     hbm = pl.BlockSpec(memory_space=pltpu.HBM)
     dma = pltpu.SemaphoreType.DMA
     tiles = sum(TILES)
-    params = dict(vmem_limit_bytes=62 * 2**20, has_side_effects=True)
+    params = dict(vmem_limit_bytes=48 * 2**20, has_side_effects=True)
     if comm:
         params["collective_id"] = 0
     return pl.pallas_call(
@@ -394,10 +434,10 @@
             pltpu.VMEM((2, tiles, BEAMS, LANES), BF16),
             pltpu.VMEM((2, tiles, BLOCK, LANES), F32),
             pltpu.VMEM((2, tiles, BLOCK, LANES), F32),
-            pltpu.VMEM((2, 8, BLOCK, 512 + LANES), BF16),
-            pltpu.VMEM((2, 4, BLOCK, 1024 + LANES), BF16),
-            pltpu.VMEM((2, 2, BLOCK, 2048 + LANES), BF16),
-            pltpu.VMEM((SLOTS, 8, 2, 2, BLOCK + GROUP, LANES), F32),
+            pltpu.VMEM((2, 8, 64, 512 + LANES), BF16),
+            pltpu.VMEM((2, 4, 64, 1024 + LANES), BF16),
+            pltpu.VMEM((2, 2, 64, 2048 + LANES), BF16),
+            pltpu.VMEM((SLOTS, 8, 2, 2, 40, LANES), F32),
             dma,
             dma((len(tables),)),
             dma((CHIPS,)),
@@ -412,6 +452,7 @@
 
 def local(images, *tables):
     grouped = images.reshape(2, 2, STRIP // GROUP, GROUP, BEAMS)
+    grouped, *tables = (pltpu.with_memory_space_constraint(x, pltpu.HBM) for x in (grouped, *tables))
     return call(grouped, tables).reshape(2, 1, 1, TILE, 4096)
 
 

time: 36 us -> 31.2 us (0.87)
  Pallas kernels: 34 us -> 30.3 us
  local copies, waits for them, and re-layouts: 1.87 us -> 0.8 us
    pallas_call x1, Pallas kernels: 34 us -> 30.3 us  [call(): pl.pallas_call(functools.partial(kernel, comm=comm, place=place), out_sha...]
    unnamed x1, local copies, waits for them, and re-layouts: 1.87 us -> 0.8 us
where the time goes in v3:
time: 31.2 us; the launch traced here: 31.1 us
  Pallas kernels  30.3 us (97%)
  local copies, waits for them, and re-layouts  0.8 us (3%)
    pallas_call x1, Pallas kernels, call(): pl.pallas_call(functools.partial(kernel, comm=comm, place=place), out_sha...  30.3 us
    unnamed x1, local copies, waits for them, and re-layouts  0.8 us

profile of v3, /device:TPU:1, one launch (start us, length us, event | category | flops | bytes accessed | tf_op | source)
XLA Modules:
  0.0 31.1 jit_solution(17595061607422122307)
XLA Ops:
  0.0 30.3 %shard_map.64 = bf16[2,32,4096]{2,1,0:T(8,128)(2,1)S(1)} custom-call(bf16[2,2,32,8,256]{4,3,2,1,0:T(8,128)(2,1)} %bitcast.5, s32[2,7680]{1,0:T(2,128)} %idx_h.1, s32[2,7680]{1,0:T(2,128)} %shf_h.1, bf16[2,4,7680]{2,1,0:T(4,128)(2,1)} %wts_h.1, f32[2,7680]{1,0:T(2,128)} %base_h.1, f32[2,7680]{1,0:T(2,128)} %slope_h.1), custom_call_target="tpu_custom_call" | custom-call | tf_op jit(solution)/shard_map/pallas_call | solution.py:425
  30.3 0.8 %copy.9 = bf16[2,1,1,32,4096]{4,3,2,1,0:T(8,128)(2,1)} copy(bf16[2,1,1,32,4096]{4,3,2,1,0:T(8,128)(2,1)S(1)} %bitcast.4) | data formatting | bytes 1048576

commit v4 on v3

--- a/solution.py
+++ b/solution.py
@@ -27,8 +27,8 @@
 ROWS = (48, 40, 40, 32)
 BASE = (-6, -4, -2, 0)
 BAND_ROWS = 96
+MARGINS = ((4, 1, 7, 2), (0, 6, 3, 5))
 STEPS = (3, 5, 2, 6, 1, 7)
-SLOTS = 4
 
 
 def build_tables(z, q, idx, shf, wts, base, slope, band, cos_t, sin_t, sections):
@@ -156,9 +156,7 @@
         for k, image in enumerate(images):
 
             def store(plane, rows, value, t=t, image=image):
-                out[plane, image, rows, (t + 1) * LANES : (t + 2) * LANES] = value
-                if t == 3:
-                    out[plane, image, rows, 0:LANES] = value
+                out[plane, image, rows, t * LANES : (t + 1) * LANES] = value
 
             combine(0, part, row0, v, slot_of(k, t), masks, cos_t, sin_t, t, store)
 
@@ -166,61 +164,64 @@
 def section_later(section, part, row0, source, shf, band, cos_t, sin_t, v, out):
     images = 8 >> section
     tiles = TILES[section]
-    half = slice(part * 32, part * 32 + 32)
+    rows = 32
+    half = slice(part * 32, part * 32 + rows)
+
+    blocks = tiles // 2
 
     def tiles_of(block):
-        return (lax.rem(2 * block + tiles - 1, tiles), 2 * block)
-
-    def multiply(slot, block):
-        window = pl.ds(pl.multiple_of(block * LANES, LANES), BEAMS)
+        return ((2 * block - 1) % tiles, 2 * block)
+
+    def slot_of(block, image, side):
+        n = (block * images + image) * 2 + side
+        return (n // 8, n % 8)
+
+    def multiply(block):
         here = tiles_of(block)
         for child in range(2):
-            lhs = source[:, child * images : (child + 1) * images, half, window]
-            lhs = lhs.reshape(2 * images * 32, BEAMS)
+            members = slice(child * images, (child + 1) * images)
+            halves = [
+                source[:, members, half, t * LANES : (t + 1) * LANES]
+                for t in ((block - 1) % blocks, block)
+            ]
+            lhs = jnp.concatenate(halves, axis=3)
+            lhs = lhs.reshape(2 * images * rows, BEAMS)
             rhs = jnp.concatenate([band[child, FIRST[section] + t] for t in here], axis=1)
             product = jnp.dot(lhs, rhs, preferred_element_type=F32)
             for plane in range(2):
                 for image in range(images):
-                    at = (plane * images + image) * 32
+                    at = (plane * images + image) * rows
                     for side in range(2):
-                        v[slot, 2 * image + side, child, plane, 0:32, :] = product[
-                            at : at + 32, side * LANES : (side + 1) * LANES
-                        ]
-
-    def finish(slot, block):
+                        to = (*slot_of(block, image, side), child, plane, slice(0, rows), slice(None))
+                        v[to] = product[at : at + rows, side * LANES : (side + 1) * LANES]
+
+    def finish(block):
         for side, t in enumerate(tiles_of(block)):
             tile = FIRST[section] + t
             masks = masks_of(shf, tile)
+            cols = slice(t * LANES, (t + 1) * LANES)
             for image in range(images):
 
-                def store(plane, rows, value, t=t, image=image):
+                def store(plane, rows, value, cols=cols, image=image):
                     if section == 3:
-                        cols = pl.ds(pl.multiple_of(t * LANES, LANES), LANES)
                         out[plane, rows, cols] = value
                     else:
-                        cols = pl.ds(pl.multiple_of((t + 1) * LANES, LANES), LANES)
                         out[plane, image, rows, cols] = value
 
-                slots = (slot, 2 * image + side)
+                slots = slot_of(block, image, side)
                 combine(section, part, row0, v, slots, masks, cos_t, sin_t, tile, store)
 
-    def body(turn, carry):
-        first = turn * SLOTS
-        multiply(0, first)
-        for slot in range(1, SLOTS):
-            multiply(slot, first + slot)
-            finish(slot - 1, first + slot - 1)
-        finish(SLOTS - 1, first + SLOTS - 1)
-        return carry
-
-    lax.fori_loop(0, tiles // 2 // SLOTS, body, 0)
-    if section < 3:
-        out[:, :, half, 0:LANES] = out[:, :, half, tiles * LANES : (tiles + 1) * LANES]
+    order = [*range(1, blocks), 0]
+    multiply(order[0])
+    for now, later in zip(order, order[1:]):
+        multiply(later)
+        finish(now)
+    finish(order[-1])
 
 
 def kernel(
     images, idx_h, shf_h, wts_h, base_h, slope_h, final,
-    recv, relay, idx, shf, wts, base, slope, band, cos_t, sin_t, s1, s2, s3, v,
+    recv, relay, idx, shf, wts, base, slope, band, cos_t, sin_t, s1, s2, s3, v0, v1, v2, v3,
     local_sem, table_sem, send_sem, recv_sem, relay_sem, forward_sem, margin_sem, comm=True, place=None,
 ):
     if comm:
@@ -368,37 +369,32 @@
                 def _(side=side):
                     margin_copy(side, image).start()
 
-        section_zero([image], 0, row0, recv, shf, band, cos_t, sin_t, v, s1)
+        section_zero([image], 0, row0, recv, shf, band, cos_t, sin_t, v0, s1)
         return carry
 
-    def margins(image, carry):
+    def outer(images):
         if comm:
-
-            @pl.when(has_previous)
-            def _():
-                margin_copy(0, image).wait_recv()
-
-            @pl.when(has_next)
-            def _():
-                margin_copy(1, image).wait_recv()
-
-        return carry
-
-    def outer(turn, carry):
-        images = [turn * 4 + k for k in range(4)]
-        section_zero(images, 1, row0, recv, shf, band, cos_t, sin_t, v, s1)
-        return carry
-
-    arrays = (s1, s2, s3, final)
-    for part in range(2):
-        if part == 0:
-            lax.fori_loop(0, CHIPS, arrival, 0)
-        else:
-            lax.fori_loop(0, CHIPS, margins, 0)
-            lax.fori_loop(0, CHIPS // 4, outer, 0)
-        for section in range(1, 4):
-            source, out = arrays[section - 1 : section + 1]
+            for image in images:
+
+                @pl.when(has_previous)
+                def _(image=image):
+                    margin_copy(0, image).wait_recv()
+
+                @pl.when(has_next)
+                def _(image=image):
+                    margin_copy(1, image).wait_recv()
+
+        section_zero(images, 1, row0, recv, shf, band, cos_t, sin_t, v0, s1)
+
+    def later(part):
+        for section, source, v, out in ((1, s1, v1, s2), (2, s2, v2, s3), (3, s3, v3, final)):
             section_later(section, part, row0, source, shf, band, cos_t, sin_t, v, out)
+
+    lax.fori_loop(0, CHIPS, arrival, 0)
+    later(0)
+    for turn in MARGINS:
+        outer([(z + CHIPS - step) % CHIPS for step in turn])
+    later(1)
 
     if comm:
         for way in range(2):
@@ -434,10 +430,10 @@
             pltpu.VMEM((2, tiles, BEAMS, LANES), BF16),
             pltpu.VMEM((2, tiles, BLOCK, LANES), F32),
             pltpu.VMEM((2, tiles, BLOCK, LANES), F32),
-            pltpu.VMEM((2, 8, 64, 512 + LANES), BF16),
-            pltpu.VMEM((2, 4, 64, 1024 + LANES), BF16),
-            pltpu.VMEM((2, 2, 64, 2048 + LANES), BF16),
-            pltpu.VMEM((SLOTS, 8, 2, 2, 40, LANES), F32),
+            pltpu.VMEM((2, 8, 64, 512), BF16),
+            pltpu.VMEM((2, 4, 64, 1024), BF16),
+            pltpu.VMEM((2, 2, 64, 2048), BF16),
+            *[pltpu.VMEM((4, 8, 2, 2, count, LANES), F32) for count in (40, 40, 40, 40)],
             dma,
             dma((len(tables),)),
             dma((CHIPS,)),

time: 31.2 us -> 30 us (0.962)
  Pallas kernels: 30.3 us -> 29.1 us
    pallas_call x1, Pallas kernels: 30.3 us -> 29.1 us  [call(): pl.pallas_call(functools.partial(kernel, comm=comm, place=place), out_sha...]
where the time goes in v4:
time: 30 us; the launch traced here: 29.9 us
  Pallas kernels  29.1 us (97%)
  local copies, waits for them, and re-layouts  0.8 us (3%)
    pallas_call x1, Pallas kernels, call(): pl.pallas_call(functools.partial(kernel, comm=comm, place=place), out_sha...  29.1 us
    unnamed x1, local copies, waits for them, and re-layouts  0.8 us

profile of v4, /device:TPU:1, one launch (start us, length us, event | category | flops | bytes accessed | tf_op | source)
XLA Modules:
  0.0 29.9 jit_solution(13333063144730153722)
XLA Ops:
  0.0 29.1 %shard_map.64 = bf16[2,32,4096]{2,1,0:T(8,128)(2,1)S(1)} custom-call(bf16[2,2,32,8,256]{4,3,2,1,0:T(8,128)(2,1)} %bitcast.5, s32[2,7680]{1,0:T(2,128)} %idx_h.1, s32[2,7680]{1,0:T(2,128)} %shf_h.1, bf16[2,4,7680]{2,1,0:T(4,128)(2,1)} %wts_h.1, f32[2,7680]{1,0:T(2,128)} %base_h.1, f32[2,7680]{1,0:T(2,128)} %slope_h.1), custom_call_target="tpu_custom_call" | custom-call | tf_op jit(solution)/shard_map/pallas_call | solution.py:421
  29.1 0.8 %copy.9 = bf16[2,1,1,32,4096]{4,3,2,1,0:T(8,128)(2,1)} copy(bf16[2,1,1,32,4096]{4,3,2,1,0:T(8,128)(2,1)S(1)} %bitcast.4) | data formatting | bytes 1048576

commit v5 on v4

--- a/solution.py
+++ b/solution.py
@@ -27,8 +27,8 @@
 ROWS = (48, 40, 40, 32)
 BASE = (-6, -4, -2, 0)
 BAND_ROWS = 96
-MARGINS = ((4, 1, 7, 2), (0, 6, 3, 5))
-STEPS = (3, 5, 2, 6, 1, 7)
+MARGINS = ((4, 2, 6, 0), (1, 7, 3, 5))
+STEPS = (3, 5, 1, 7, 2, 6)
 
 
 def build_tables(z, q, idx, shf, wts, base, slope, band, cos_t, sin_t, sections):
@@ -161,7 +161,7 @@
             combine(0, part, row0, v, slot_of(k, t), masks, cos_t, sin_t, t, store)
 
 
-def section_later(section, part, row0, source, shf, band, cos_t, sin_t, v, out):
+def section_later(section, part, chosen, row0, source, shf, band, cos_t, sin_t, v, out):
     images = 8 >> section
     tiles = TILES[section]
     rows = 32
@@ -173,24 +173,30 @@
         return ((2 * block - 1) % tiles, 2 * block)
 
     def slot_of(block, image, side):
-        n = (block * images + image) * 2 + side
+        n = (block * len(chosen) + image) * 2 + side
         return (n // 8, n % 8)
 
     def multiply(block):
         here = tiles_of(block)
         for child in range(2):
-            members = slice(child * images, (child + 1) * images)
-            halves = [
-                source[:, members, half, t * LANES : (t + 1) * LANES]
-                for t in ((block - 1) % blocks, block)
-            ]
-            lhs = jnp.concatenate(halves, axis=3)
-            lhs = lhs.reshape(2 * images * rows, BEAMS)
+            lhs = jnp.concatenate(
+                [
+                    jnp.concatenate(
+                        [
+                            source[:, child * images + image, half, t * LANES : (t + 1) * LANES]
+                            for t in ((block - 1) % blocks, block)
+                        ],
+                        axis=2,
+                    )
+                    for image in chosen
+                ],
+                axis=1,
+            ).reshape(2 * len(chosen) * rows, BEAMS)
             rhs = jnp.concatenate([band[child, FIRST[section] + t] for t in here], axis=1)
             product = jnp.dot(lhs, rhs, preferred_element_type=F32)
             for plane in range(2):
-                for image in range(images):
-                    at = (plane * images + image) * rows
+                for image in range(len(chosen)):
+                    at = (plane * len(chosen) + image) * rows
                     for side in range(2):
                         to = (*slot_of(block, image, side), child, plane, slice(0, rows), slice(None))
                         v[to] = product[at : at + rows, side * LANES : (side + 1) * LANES]
@@ -200,7 +206,7 @@
             tile = FIRST[section] + t
             masks = masks_of(shf, tile)
             cols = slice(t * LANES, (t + 1) * LANES)
-            for image in range(images):
+            for k, image in enumerate(chosen):
 
                 def store(plane, rows, value, cols=cols, image=image):
                     if section == 3:
@@ -208,7 +214,7 @@
                     else:
                         out[plane, image, rows, cols] = value
 
-                slots = slot_of(block, image, side)
+                slots = slot_of(block, k, side)
                 combine(section, part, row0, v, slots, masks, cos_t, sin_t, tile, store)
 
     order = [*range(1, blocks), 0]
@@ -222,7 +228,7 @@
 def kernel(
     images, idx_h, shf_h, wts_h, base_h, slope_h, final,
     recv, relay, idx, shf, wts, base, slope, band, cos_t, sin_t, s1, s2, s3, v0, v1, v2, v3,
-    local_sem, table_sem, send_sem, recv_sem, relay_sem, forward_sem, margin_sem, comm=True, place=None,
+    local_sem, table_sem, send_sem, recv_sem, relay_sem, forward_sem, margin_sem, edge_sem, comm=True, place=None,
 ):
     if comm:
         sub, q = lax.axis_index("sub"), lax.axis_index("rng")
@@ -250,11 +256,17 @@
             )
         leaves_up = (z == CHIPS - 1) & (q < STRIPS - 1)
         leaves_down = (z == 0) & (q > 0)
-        for side, leaves in enumerate((leaves_up, leaves_down)):
-
-            @pl.when(leaves)
-            def _(side=side):
-                pl.semaphore_signal(barrier, inc=1, device_id=beside(side), device_id_type=MESH)
+
+        @pl.when(leaves_up)
+        def _():
+            pl.semaphore_signal(barrier, inc=1, device_id=beside(0), device_id_type=MESH)
+
+        @pl.when(leaves_down)
+        def _():
+            for other in range(CHIPS):
+                pl.semaphore_signal(
+                    barrier, inc=1, device_id=device(other, q - 1), device_id_type=MESH
+                )
 
     fetches = [
         pltpu.make_async_copy(src, dst, table_sem.at[i])
@@ -275,7 +287,8 @@
             images.at[:, :, of_tile(z)], recv.at[z, :, :, main], local_sem
         )
         own.start()
-        peers = CHIPS - 1 + leaves_up.astype(jnp.int32) + leaves_down.astype(jnp.int32)
+        below = q < STRIPS - 1
+        peers = CHIPS - 1 + below.astype(jnp.int32) + leaves_down.astype(jnp.int32)
         pl.semaphore_wait(barrier, peers)
 
         def block_copy(step):
@@ -319,6 +332,20 @@
                 device_id_type=MESH,
             )
 
+        def edge_copy():
+            return pltpu.make_async_remote_copy(
+                src_ref=images.at[:, :, STRIP // GROUP - 1],
+                dst_ref=recv.at[z, :, :, 0],
+                send_sem=edge_sem,
+                recv_sem=margin_sem.at[1, 0, z],
+                device_id=device(0, q + 1),
+                device_id_type=MESH,
+            )
+
+        @pl.when(below)
+        def _():
+            edge_copy().start()
+
         for way in range(2):
             relay_copy(way).start()
         for step in STEPS:
@@ -348,9 +375,9 @@
     row0 = q * STRIP + z * TILE
 
     def arrival(turn, carry):
-        far = 3 - (turn - 1) // 2
-        step = jnp.where(turn % 2 == 1, far, CHIPS - far)
-        step = jnp.where(turn == 0, 0, jnp.where(turn == CHIPS - 1, 4, step))
+        step = jnp.int32(0)
+        for position, distance in enumerate((*STEPS, 4)):
+            step = jnp.where(turn == position + 1, distance, step)
         image = (z + CHIPS - step) % CHIPS
         if comm:
 
@@ -363,7 +390,7 @@
                 for way in range(2):
                     forward_copy(way).wait_recv()
 
-            for side, there in enumerate((has_next, has_previous)):
+            for side, there in ((1, has_previous), (0, z < CHIPS - 1)):
 
                 @pl.when(there)
                 def _(side=side):
@@ -386,15 +413,23 @@
 
         section_zero(images, 1, row0, recv, shf, band, cos_t, sin_t, v0, s1)
 
-    def later(part):
-        for section, source, v, out in ((1, s1, v1, s2), (2, s2, v2, s3), (3, s3, v3, final)):
-            section_later(section, part, row0, source, shf, band, cos_t, sin_t, v, out)
-
-    lax.fori_loop(0, CHIPS, arrival, 0)
-    later(0)
+    def merge(section, part, chosen):
+        source, v, out = ((s1, v1, s2), (s2, v2, s3), (s3, v3, final))[section - 1]
+        section_later(section, part, chosen, row0, source, shf, band, cos_t, sin_t, v, out)
+
+    lax.fori_loop(0, 5, arrival, 0)
+    merge(1, 0, [(z + 7) % 4, (z + 5) % 4])
+    merge(2, 0, [(z + 7) % 2])
+    lax.fori_loop(5, 7, arrival, 0)
+    merge(1, 0, [(z + 6) % 4])
+    lax.fori_loop(7, 8, arrival, 0)
+    merge(1, 0, [z % 4])
+    merge(2, 0, [z % 2])
+    merge(3, 0, [0])
     for turn in MARGINS:
         outer([(z + CHIPS - step) % CHIPS for step in turn])
-    later(1)
+    for section in range(1, 4):
+        merge(section, 1, list(range(8 >> section)))
 
     if comm:
         for way in range(2):
@@ -402,12 +437,16 @@
             forward_copy(way).wait_send()
         for step in STEPS:
             block_copy(step).wait_send()
-        for side, there in enumerate((has_next, has_previous)):
+        for side, there in ((1, has_previous), (0, z < CHIPS - 1)):
 
             @pl.when(there)
             def _(side=side):
                 for image in range(CHIPS):
                     margin_copy(side, image).wait_send()
+
+        @pl.when(below)
+        def _():
+            edge_copy().wait_send()
 
 
 def call(images, tables, comm=True, place=None):
@@ -441,6 +480,7 @@
             dma((2, 2)),
             dma((2, 2)),
             dma((2, 2, CHIPS)),
+            dma,
         ],
         compiler_params=pltpu.CompilerParams(**params),
     )(images, *tables)

time: 30 us -> 29.5 us (0.983)
  the two profiles are of different devices: /device:TPU:1 before, /device:TPU:8 now
where the time goes in v5:
time: 29.5 us; the launch traced here: 29.4 us
  Pallas kernels  28.6 us (97%)
  local copies, waits for them, and re-layouts  0.8 us (3%)
    pallas_call x1, Pallas kernels, call(): pl.pallas_call(functools.partial(kernel, comm=comm, place=place), out_sha...  28.6 us
    unnamed x1, local copies, waits for them, and re-layouts  0.8 us

profile of v5, /device:TPU:8, one launch (start us, length us, event | category | flops | bytes accessed | tf_op | source)
XLA Modules:
  0.0 29.4 jit_solution(9731514239967144697)
XLA Ops:
  0.0 28.6 %shard_map.64 = bf16[2,32,4096]{2,1,0:T(8,128)(2,1)S(1)} custom-call(bf16[2,2,32,8,256]{4,3,2,1,0:T(8,128)(2,1)} %bitcast.5, s32[2,7680]{1,0:T(2,128)} %idx_h.1, s32[2,7680]{1,0:T(2,128)} %shf_h.1, bf16[2,4,7680]{2,1,0:T(4,128)(2,1)} %wts_h.1, f32[2,7680]{1,0:T(2,128)} %base_h.1, f32[2,7680]{1,0:T(2,128)} %slope_h.1), custom_call_target="tpu_custom_call" | custom-call | tf_op jit(solution)/shard_map/pallas_call | solution.py:460
  28.6 0.8 %copy.9 = bf16[2,1,1,32,4096]{4,3,2,1,0:T(8,128)(2,1)} copy(bf16[2,1,1,32,4096]{4,3,2,1,0:T(8,128)(2,1)S(1)} %bitcast.4) | data formatting | bytes 1048576
